TPU v7x, 32 devices: a whole 2x2x4 slice. The times are simulated.
32 devices in a mesh: grp: 2 (over x), row: 8 (over z, y), col: 2 (over core).
Axes of the slice: x: 2, y: 2, z: 4, core: 2. Of those that a mesh axis runs over, the one named last changes fastest.
Arguments:
- score_panel: bfloat16 [2, 8, 2, 512, 128], P('grp', 'row', 'col'), parts along dimension 0, may hold values from -6 to 6
- blocks: bfloat16 [8, 2, 8, 512, 512], P('row', 'col'), may hold values from -0.09375 to 0.09375
- block_rows: int32 [8, 2, 8], P('row', 'col'), may hold values from 0 to 15, as said below
- block_cols: int32 [8, 2, 8], P('row', 'col'), may hold values from 0 to 15, as said below
- counts: int32 [8, 2], P('row', 'col'), may hold values from 1 to 8, as said below
- degrees: int32 [1, 8, 2, 512], replicated, may hold values from 1 to 4
Outputs:
- scores: bfloat16 [2, 8, 2, 512, 128], P('grp', 'row', 'col'), parts along dimension 0
There are 2 independent parts, one for each index of `grp`. A program takes and returns all parts, laid end to end along the dimension named above; an argument that names none is the same for every part. Nothing has to cross between parts.
Inputs may be any that keep to these rules, and one draw needn't show every extreme that they name: `block_rows`: slot k of the cell with row index r and column index c names a block b with (b // 2) % 8 == r; below counts it is at most block_cols of that slot; pairs in a cell are distinct. `block_cols`: slot k of the cell with column index c names a block b with b % 2 == c; slots at or after counts name blocks of the same sets and carry no weight. `counts`: used slots come first in each cell; every cell uses at least one slot.
All inputs are finite; a program needn't handle non-finite values.
Results may differ from a plain program's by a relative error of at most 0.0041.
Values may be sent and summed in bfloat16 or wider, within the bound.
A program may use at most 64 MiB of HBM per device.

v0:
```python
import jax
import jax.numpy as jnp
from jax import lax
from jax.sharding import PartitionSpec as P


def column_total(col_part):
    return lax.psum_scatter(col_part, "row", scatter_dimension=1, tiled=True)


def shards(score_panel, blocks, block_rows, block_cols, counts, degrees):
    stacks = score_panel.shape[0]
    block_edge = score_panel.shape[3]
    user_count = score_panel.shape[4]
    row_count = lax.axis_size("row")
    col_count = lax.axis_size("col")
    row_index = lax.axis_index("row")
    col_index = lax.axis_index("col")
    slot_total = blocks.shape[2]
    tile_set = blocks.reshape(slot_total, block_edge, block_edge)
    row_ids = block_rows.reshape(slot_total)
    col_ids = block_cols.reshape(slot_total)
    in_use = jnp.arange(slot_total) < counts.reshape(())
    weight = jnp.where(in_use, jnp.where(row_ids == col_ids, 0.5, 1.0), 0.0).astype(jnp.float32)
    row_local = row_ids // (row_count * col_count) * col_count + row_ids % col_count
    col_local = col_ids // col_count
    row_onehot = (jnp.arange(stacks * col_count)[:, None] == row_local[None, :]).astype(
        jnp.float32
    ) * weight[None, :]
    col_onehot = (jnp.arange(stacks * row_count)[:, None] == col_local[None, :]).astype(
        jnp.float32
    ) * weight[None, :]
    inv_all = lax.rsqrt(degrees.astype(jnp.float32))
    col_inv = lax.dynamic_slice_in_dim(inv_all, col_index, 1, 2).reshape(
        stacks * row_count, block_edge, 1
    )
    own_inv = lax.dynamic_slice_in_dim(
        col_inv.reshape(stacks, row_count, block_edge, 1), row_index, 1, 1
    )
    own_inv = own_inv.reshape(stacks, 1, 1, block_edge, 1)

    def local_terms(row_set, col_set):
        col_pick = jnp.take(col_set, col_local, axis=0)
        row_pick = jnp.take(row_set, row_local, axis=0)
        forward = jnp.einsum("kab,kbu->kau", tile_set, col_pick, preferred_element_type=jnp.float32)
        backward = jnp.einsum(
            "kab,kau->kbu", tile_set, row_pick, preferred_element_type=jnp.float32
        )
        row_part = jnp.dot(
            row_onehot, forward.reshape(slot_total, -1), precision=lax.Precision.HIGHEST
        )
        col_part = jnp.dot(
            col_onehot, backward.reshape(slot_total, -1), precision=lax.Precision.HIGHEST
        )
        return (
            row_part.reshape(stacks, col_count, block_edge, user_count),
            col_part.reshape(stacks, row_count, block_edge, user_count),
        )

    def row_set_of(own_sent):
        return lax.all_gather(own_sent, "col", axis=2, tiled=True).reshape(
            stacks * col_count, block_edge, user_count
        )

    def row_total(row_part):
        return lax.psum_scatter(row_part, "col", scatter_dimension=1, tiled=True)

    sent_first = (own_inv * score_panel.astype(jnp.float32)).astype(jnp.bfloat16)
    col_set = lax.all_gather(sent_first, "row", axis=1, tiled=True).reshape(
        stacks * row_count, block_edge, user_count
    )
    row_part, col_part = local_terms(row_set_of(sent_first), col_set)
    row_own = row_total(row_part)
    col_own = column_total(col_part)
    first = own_inv * (col_own + row_own)[:, :, None]
    sent_second = (own_inv * first).astype(jnp.bfloat16)
    col_set = lax.all_gather(sent_second, "row", axis=1, tiled=True).reshape(
        stacks * row_count, block_edge, user_count
    )
    row_part, col_part = local_terms(row_set_of(sent_second), col_set)
    row_own = row_total(row_part)
    col_own = column_total(col_part)
    scores = first + own_inv * (col_own + row_own)[:, :, None]
    return scores.astype(jnp.bfloat16)


def solution(mesh):
    in_specs = (
        P("grp", "row", "col", None, None),
        P("row", "col", None, None, None),
        P("row", "col", None),
        P("row", "col", None),
        P("row", "col"),
        P(),
    )
    out_specs = P("grp", "row", "col", None, None)
    return jax.shard_map(shards, mesh=mesh, in_specs=in_specs, out_specs=out_specs, check_vma=False)
```

profile of v0, /device:TPU:1, one launch (start us, length us, event | category | flops | bytes accessed | tf_op | source)
XLA Modules:
  0.0 287.8 jit_solution(13337364610593953938)
XLA Ops:
  6.5 0.0 all-gather.3.cloned.1.call-start
  6.5 0.7 fusion.51
  7.2 1.7 fusion.77
  8.9 0.0 all-gather.3.cloned.1.call-update
  9.0 0.0 reduce-scatter.7.cloned.1.call-start
  9.7 0.7 compare_and_fusion
  10.3 0.7 compare_and_fusion.1
  11.0 0.7 compare_select_fusion.4
  11.7 39.0 %all-gather.3.cloned.1.call-done = bf16[1,8,1,512,128]{4,3,2,0,1:T(8,128)(2,1)} async-done(((bf16[1,1,1,512,128]{4,3,2,0,1:T(8,128)(2,1)}), bf16[1,8,1,512,128]{4,3,2,0,1:T(8,128)(2,1)}) %all-gather.3.cloned.1.call-update) | async-done | bytes 1048592 | tf_op jit(solution)/shard_map/all_gather | solution.py:69
  50.7 2.0 gather_fusion.1
  52.7 5.3 %fusion.21 = f32[8,512,128]{1,2,0:T(8,128)} fusion(bf16[1,1,8,512,512]{4,3,2,1,0:T(8,128)(2,1)} %param.11, bf16[8,512,128]{2,1,0:T(8,128)(2,1)S(1)} %gather_fusion.1, pred[8]{0:T(512)(128)(4,1)S(1)} %get-tuple-element.9), kind=kOutput, calls=%fused_computation.27 | convolution fusion | flops 537395200 | bytes 7340040 | tf_op jit(solution)/shard_map/kab,kbu->kau/dot_general | solution.py:45
  58.0 1.9 copy.45
  59.9 0.0 copy-start.3
  59.9 2.8 fusion.30
  62.8 0.8 copy.46
  63.6 0.0 reduce-scatter.7.cloned.1.call-update
  63.6 0.0 reduce-scatter.5.cloned.1.call-start
  63.7 0.0 copy-done.3
  63.7 0.1 multiply_convert_fusion.1
  63.8 3.3 %all_gather.12 = bf16[1,1,2,512,128]{4,3,1,0,2:T(8,128)(2,1)S(1)} all-gather(bf16[1,1,1,512,128]{4,3,1,0,2:T(8,128)(2,1)S(1)} %multiply_convert_fusion.1), channel_id=1, replica_groups=mesh['grp'=2,'row'=8,'col'=2] {'col'}, dimensions={2}, use_global_device_ids=true | all-gather | bytes 393216 | tf_op jit(solution)/shard_map/all_gather | solution.py:61
  67.1 0.7 gather_fusion
  67.9 4.6 %fusion.18 = f32[8,512,128]{1,2,0:T(8,128)} fusion(bf16[1,1,8,512,512]{4,3,2,1,0:T(8,128)(2,1)} %param.11, bf16[8,512,128]{2,1,0:T(8,128)(2,1)S(1)} %gather_fusion, pred[8]{0:T(512)(128)(4,1)S(1)} %get-tuple-element.6), kind=kOutput, calls=%fused_computation.26 | convolution fusion | flops 537395200 | bytes 7340040 | tf_op jit(solution)/shard_map/kab,kau->kbu/dot_general | solution.py:46
  72.6 1.9 copy.41
  74.5 2.9 fusion.16
  77.3 1.7 copy.42
  79.0 0.0 reduce-scatter.5.cloned.1.call-update
  79.1 0.0 all-gather.5.cloned.1.call-start
  79.1 0.0 reduce-scatter.7.cloned.1.call-done
  79.1 64.5 %reduce-scatter.5.cloned.1.call-done = f32[1,1,512,128]{3,2,0,1:T(8,128)} async-done(((f32[1,8,512,128]{3,2,0,1:T(8,128)}), f32[1,1,512,128]{3,2,0,1:T(8,128)}) %reduce-scatter.5.cloned.1.call-update) | async-done | bytes 262160 | tf_op jit(solution)/shard_map/reduce_scatter | solution.py:8
  143.7 1.8 multiply_convert_fusion
  145.5 0.0 all-gather.5.cloned.1.call-update
  145.5 0.2 reduce-scatter.11.cloned.1.call-start
  145.8 40.1 %all-gather.5.cloned.1.call-done = bf16[1,8,1,512,128]{4,3,2,0,1:T(8,128)(2,1)} async-done(((bf16[1,1,1,512,128]{4,3,2,0,1:T(8,128)(2,1)}), bf16[1,8,1,512,128]{4,3,2,0,1:T(8,128)(2,1)}) %all-gather.5.cloned.1.call-update) | async-done | bytes 1048592 | tf_op jit(solution)/shard_map/all_gather | solution.py:77
  185.9 2.0 gather_fusion.3
  187.9 5.3 %fusion.27 = f32[8,512,128]{1,2,0:T(8,128)} fusion(bf16[1,1,8,512,512]{4,3,2,1,0:T(8,128)(2,1)} %param.11, bf16[8,512,128]{2,1,0:T(8,128)(2,1)S(1)} %gather_fusion.3, pred[8]{0:T(512)(128)(4,1)S(1)} %get-tuple-element.9), kind=kOutput, calls=%fused_computation.29 | convolution fusion | flops 537395200 | bytes 7340040 | tf_op jit(solution)/shard_map/kab,kbu->kau/dot_general | solution.py:45
  193.2 1.9 copy.54
  195.1 0.0 copy-start
  195.1 2.8 fusion.31
  197.9 0.8 copy.55
  198.8 0.0 reduce-scatter.11.cloned.1.call-update
  198.8 0.0 reduce-scatter.9.cloned.1.call-start
  198.8 0.0 copy-done
  198.8 3.3 %all_gather.14 = bf16[1,1,2,512,128]{4,3,1,0,2:T(8,128)(2,1)S(1)} all-gather(bf16[1,1,1,512,128]{4,3,1,0,2:T(8,128)(2,1)S(1)} %copy-done), channel_id=1, replica_groups=mesh['grp'=2,'row'=8,'col'=2] {'col'}, dimensions={2}, use_global_device_ids=true | all-gather | bytes 393216 | tf_op jit(solution)/shard_map/all_gather | solution.py:61
  202.2 0.7 gather_fusion.2
  202.9 4.6 %fusion.24 = f32[8,512,128]{1,2,0:T(8,128)} fusion(bf16[1,1,8,512,512]{4,3,2,1,0:T(8,128)(2,1)} %param.11, bf16[8,512,128]{2,1,0:T(8,128)(2,1)S(1)} %gather_fusion.2, pred[8]{0:T(512)(128)(4,1)S(1)} %get-tuple-element.6), kind=kOutput, calls=%fused_computation.28 | convolution fusion | flops 537395200 | bytes 7340040 | tf_op jit(solution)/shard_map/kab,kau->kbu/dot_general | solution.py:46
  207.5 1.9 copy.50
  209.4 2.9 fusion.17
  212.3 1.7 copy.51
  214.0 0.0 copy-start.1
  214.0 0.0 copy-start.2
  214.0 0.0 reduce-scatter.9.cloned.1.call-update
  214.0 0.0 reduce-scatter.11.cloned.1.call-done
  214.0 65.1 %reduce-scatter.9.cloned.1.call-done = f32[1,1,512,128]{3,2,0,1:T(8,128)} async-done(((f32[1,8,512,128]{3,2,0,1:T(8,128)}), f32[1,1,512,128]{3,2,0,1:T(8,128)}) %reduce-scatter.9.cloned.1.call-update) | async-done | bytes 262160 | tf_op jit(solution)/shard_map/reduce_scatter | solution.py:8
  279.2 0.0 copy-done.1
  279.2 0.0 copy-done.2
  279.2 1.8 fusion.46
  (4 shorter events, 0.0 us)
Async XLA Ops:
  6.5 44.2 %all-gather.3.cloned.1.call-start = ((), (), s32[]{:S(2)}) async-start(), calls=%async_computation.5 | async-start | bytes 1179648 | tf_op jit(solution)/shard_map/all_gather | solution.py:69
  9.0 70.2 %reduce-scatter.7.cloned.1.call-start = ((), (), s32[]{:S(2)}) async-start(), calls=%async_computation.6 | async-start | bytes 786432 | tf_op jit(solution)/shard_map/reduce_scatter | solution.py:66
  59.9 3.8 %copy-start.3 = (bf16[1,1,1,512,128]{4,3,2,1,0:T(8,128)(2,1)S(1)}, bf16[1,1,1,512,128]{4,3,2,1,0:T(8,128)(2,1)}, u32[]{:S(2)}) copy-start(bf16[1,1,1,512,128]{4,3,2,1,0:T(8,128)(2,1)} %param.10) | copy-start | bytes 393220
  63.6 80.1 %reduce-scatter.5.cloned.1.call-start = ((), (), s32[]{:S(2)}) async-start(), calls=%async_computation.4 | async-start | bytes 2359296 | tf_op jit(solution)/shard_map/reduce_scatter | solution.py:8
  79.1 106.8 %all-gather.5.cloned.1.call-start = ((), (), s32[]{:S(2)}) async-start(), calls=%async_computation.8 | async-start | bytes 1179648 | tf_op jit(solution)/shard_map/all_gather | solution.py:77
  145.5 68.5 %reduce-scatter.11.cloned.1.call-start = ((), (), s32[]{:S(2)}) async-start(), calls=%async_computation.9 | async-start | bytes 786432 | tf_op jit(solution)/shard_map/reduce_scatter | solution.py:66
  195.1 3.8 %copy-start = (bf16[1,1,1,512,128]{4,3,1,0,2:T(8,128)(2,1)S(1)}, bf16[1,1,1,512,128]{4,3,1,0,2:T(8,128)(2,1)}, u32[]{:S(2)}) copy-start(bf16[1,1,1,512,128]{4,3,1,0,2:T(8,128)(2,1)} %multiply_convert_fusion) | copy-start | bytes 393220
  198.8 80.4 %reduce-scatter.9.cloned.1.call-start = ((), (), s32[]{:S(2)}) async-start(), calls=%async_computation.7 | async-start | bytes 2359296 | tf_op jit(solution)/shard_map/reduce_scatter | solution.py:8
  214.0 65.2 %copy-start.1 = (f32[1,1,512,128]{3,2,0,1:T(8,128)S(1)}, f32[1,1,512,128]{3,2,0,1:T(8,128)}, u32[]{:S(2)}) copy-start(f32[1,1,512,128]{3,2,0,1:T(8,128)} %reduce-scatter.7.cloned.1.call-done) | copy-start | bytes 786436
  214.0 65.2 %copy-start.2 = (f32[1,1,512,128]{3,2,0,1:T(8,128)S(1)}, f32[1,1,512,128]{3,2,0,1:T(8,128)}, u32[]{:S(2)}) copy-start(f32[1,1,512,128]{3,2,0,1:T(8,128)} %reduce-scatter.5.cloned.1.call-done) | copy-start | bytes 786436
Sparse Core Ops, SparseCore 0:
  9.5 41.2 all-gather.2
  63.8 8.0 reduce-scatter.6
  79.2 64.4 reduce-scatter.4
  145.9 39.9 all-gather.4
  198.9 8.0 reduce-scatter.10
  214.1 65.0 reduce-scatter.8
where the time goes:
time: 290 us; the launch traced here: 288 us
  waiting for transfers between devices  209 us (72%)
  matrix products  31.1 us (11%)
  local copies, waits for them, and re-layouts  18.2 us (6%)
  between operations  14.3 us (5%)
  other arithmetic  8.21 us (3%)
  blocking collectives  6.61 us (2%)
    reduce_scatter x2, waiting for transfers between devices, column_total(): return lax.psum_scatter(col_part, 'row', scatter_dimension=1, tiled=True)  130 us
    all_gather x1, waiting for transfers between devices, shards(): lax.all_gather(sent_second, 'row', axis=1, tiled=True)  40.1 us
    all_gather x1, waiting for transfers between devices, shards(): lax.all_gather(sent_first, 'row', axis=1, tiled=True)  39 us
    dot_general x2, matrix products, local_terms(): jnp.einsum('kab,kbu->kau', tile_set, col_pick, preferred_element_type=jnp...  10.5 us
    dot_general x2, matrix products, local_terms(): jnp.einsum('kab,kau->kbu', tile_set, row_pick, preferred_element_type=jnp...  9.2 us
    all_gather x2, blocking collectives, row_set_of(): lax.all_gather(own_sent, 'col', axis=2, tiled=True)  6.61 us
  transfers between devices with their start and end apart: 6, of which 4 were waited for; matrix products, arithmetic and copies ran while one was open for 9% of the time, Pallas kernels for 0%

commit v1 on v0

v1 whole, which is shorter than its diff:
```python
import functools

import jax
import jax.numpy as jnp
from jax import lax
from jax.experimental import pallas as pl
from jax.experimental.pallas import tpu as pltpu
from jax.sharding import PartitionSpec as P

F32 = jnp.float32
BF16 = jnp.bfloat16


def kernel(
    row_count,
    slot_total,
    panel_ref,
    blocks_ref,
    rows_ref,
    cols_ref,
    counts_ref,
    degrees_ref,
    out_ref,
    tiles,
    gathered,
    mate_panel,
    y_out,
    y_in,
    z_out,
    z_in,
    own_terms,
    row_acc,
    mate_out,
    mate_in,
    first_keep,
    slot_of,
    weight_of,
    load_sem,
    gz_send,
    gz_recv,
    gy_send,
    gy_recv,
    gm_send,
    gm_recv,
    ry_send,
    ry_recv,
    rz_send,
    rz_recv,
    rm_send,
    rm_recv,
):
    r = lax.axis_index("row")
    c = lax.axis_index("col")
    z = r // 2
    y = r % 2
    levels = row_count // 2
    y_peer = r + 1 - 2 * y
    mate = 1 - c

    for k in range(slot_total):
        pltpu.make_async_copy(blocks_ref.at[0, 0, k], tiles.at[k], load_sem.at[k]).start()

    barrier = pltpu.get_barrier_semaphore()
    pl.semaphore_signal(barrier, inc=1, device_id={"col": mate})
    pl.semaphore_signal(barrier, inc=1, device_id={"row": y_peer})

    @pl.when(z > 0)
    def _():
        pl.semaphore_signal(barrier, inc=1, device_id={"row": r - 2})

    @pl.when(z < levels - 1)
    def _():
        pl.semaphore_signal(barrier, inc=1, device_id={"row": r + 2})

    pair = degrees_ref[0, r].astype(F32)
    inv = lax.rsqrt(jnp.where(c == 0, pair[0:1], pair[1:2]))
    panel = panel_ref[0, 0, 0].astype(F32).T
    gathered[0, r] = (inv * panel).astype(BF16)

    below = (z > 0).astype(jnp.int32)
    above = (z < levels - 1).astype(jnp.int32)
    pl.semaphore_wait(barrier, 2 + below + above)

    def remote(src, dst, send, recv, where):
        return pltpu.make_async_remote_copy(
            src_ref=src, dst_ref=dst, send_sem=send, recv_sem=recv, device_id=where
        )

    def gather_z(a, zp):
        ref = gathered.at[a, 2 * zp + y]
        return remote(ref, ref, gz_send.at[a, zp], gz_recv.at[a, zp], {"row": r - 2})

    def gather_y(a, zp):
        ref = gathered.at[a, 2 * zp + y]
        return remote(ref, ref, gy_send.at[a, zp], gy_recv.at[a, zp], {"row": y_peer})

    def arrive_y(a, zp):
        ref = gathered.at[a, 2 * zp + 1 - y]
        return remote(ref, ref, gy_send.at[a, zp], gy_recv.at[a, zp], {"row": y_peer})

    def gather_m(a):
        return remote(
            gathered.at[a, r], mate_panel.at[a], gm_send.at[a], gm_recv.at[a], {"col": mate}
        )

    def reduce_y(a, zp):
        return remote(
            y_out.at[a, zp], y_in.at[a, zp], ry_send.at[a, zp], ry_recv.at[a, zp], {"row": y_peer}
        )

    def reduce_z(a, zp):
        return remote(
            z_out.at[a, zp], z_in.at[a, zp], rz_send.at[a, zp], rz_recv.at[a, zp], {"row": r + 2}
        )

    def reduce_m(a):
        return remote(mate_out.at[a], mate_in.at[a], rm_send.at[a], rm_recv.at[a], {"col": mate})

    def start_gather(a):
        gather_m(a).start()

        @pl.when(z > 0)
        def _():
            gather_z(a, z).start()

        @pl.when(y == 1)
        def _():
            gather_y(a, z).start()

    start_gather(0)

    used = counts_ref[0, 0]

    def fill(rp, carry):
        for h in range(2):
            row_id = 2 * r + (c if h == 0 else mate)
            col_id = 2 * rp + c
            share = jnp.where(row_id == col_id, 0.5, 1.0).astype(F32)
            at = jnp.int32(0)
            weight = jnp.float32(0)
            for k in range(slot_total):
                hit = (rows_ref[0, 0, k] == row_id) & (cols_ref[0, 0, k] == col_id) & (k < used)
                at = jnp.where(hit, jnp.int32(k), at)
                weight = jnp.where(hit, share, weight)
            slot_of[h, rp] = at
            weight_of[h, rp] = weight
        return carry

    lax.fori_loop(r, row_count, fill, 0)

    for k in range(slot_total):
        pltpu.make_async_copy(blocks_ref.at[0, 0, k], tiles.at[k], load_sem.at[k]).wait()

    def transposed_term(a, rp):
        total = None
        for h in range(2):
            panel_h = gathered[a, r] if h == 0 else mate_panel[a]
            term = weight_of[h, rp] * jnp.dot(
                panel_h, tiles[slot_of[h, rp]], preferred_element_type=F32
            )
            total = term if total is None else total + term
        return total

    def add_forward(a, rp, fresh=False):
        for h in range(2):
            term = weight_of[h, rp] * lax.dot_general(
                gathered[a, rp],
                tiles[slot_of[h, rp]],
                (((1,), (1,)), ((), ())),
                preferred_element_type=F32,
            )
            if fresh:
                row_acc[h] = term
            else:
                row_acc[h] += term

    def apply(a):
        gather_m(a).wait_recv()

        def send_terms(s, carry):
            zp = levels - 1 - s
            y_out[a, zp] = transposed_term(a, 2 * zp + 1 - y).astype(BF16)
            reduce_y(a, zp).start()
            own_terms[zp] = transposed_term(a, 2 * zp + y)
            return carry

        lax.fori_loop(0, levels - 1 - z, send_terms, 0)

        @pl.when(y == 0)
        def _():
            y_out[a, z] = transposed_term(a, r + 1).astype(BF16)
            reduce_y(a, z).start()

        own_terms[z] = transposed_term(a, r)
        add_forward(a, r, fresh=True)

        def from_peer(zp):
            arrive_y(a, zp).wait_recv()
            add_forward(a, 2 * zp + 1 - y)

        def step(s, carry):
            zp = z + s
            gather_z(a, zp).wait_recv()

            @pl.when(z > 0)
            def _():
                gather_z(a, zp).start()

            gather_y(a, zp).start()
            zq = levels - s
            reduce_y(a, zq).wait_recv()
            summed = own_terms[zq] + y_in[a, zq].astype(F32)

            @pl.when(z > 0)
            def _():
                reduce_z(a, zq).wait_recv()
                z_out[a, zq] = (summed + z_in[a, zq].astype(F32)).astype(BF16)

            @pl.when(z == 0)
            def _():
                z_out[a, zq] = summed.astype(BF16)

            reduce_z(a, zq).start()
            add_forward(a, 2 * zp + y)

            @pl.when((s > 1) | (y == 0))
            def _():
                from_peer(zp - 1)

            return carry

        lax.fori_loop(1, levels - z, step, 0)

        @pl.when((z < levels - 1) | (y == 0))
        def _():
            from_peer(levels - 1)

        mate_out[a] = row_acc[1]
        reduce_m(a).start()
        row_acc[0] += own_terms[z]

        @pl.when(y == 1)
        def _():
            reduce_y(a, z).wait_recv()
            row_acc[0] += y_in[a, z].astype(F32)

        @pl.when(z > 0)
        def _():
            reduce_z(a, z).wait_recv()
            row_acc[0] += z_in[a, z].astype(F32)

        reduce_m(a).wait_recv()
        return inv * (row_acc[0] + mate_in[a])

    first = apply(0)
    first_keep[...] = first
    gathered[1, r] = (inv * first).astype(BF16)
    start_gather(1)
    second = apply(1)
    out_ref[0, 0, 0] = (first_keep[...] + second).T.astype(BF16)

    for a in range(2):
        gather_m(a).wait_send()
        reduce_m(a).wait_send()

        @pl.when(z > 0)
        def _():
            gather_z(a, z).wait_send()

        @pl.when(y == 1)
        def _():
            gather_y(a, z).wait_send()

        @pl.when(y == 0)
        def _():
            reduce_y(a, z).wait_send()

        def finish(zp, carry):
            @pl.when(z > 0)
            def _():
                gather_z(a, zp).wait_send()

            gather_y(a, zp).wait_send()
            reduce_y(a, zp).wait_send()
            reduce_z(a, zp).wait_send()
            return carry

        lax.fori_loop(z + 1, levels, finish, 0)


def shards(score_panel, blocks, block_rows, block_cols, counts, degrees):
    row_count = degrees.shape[1]
    levels = row_count // 2
    slot_total, edge = blocks.shape[2], blocks.shape[3]
    users = score_panel.shape[4]
    vmem = pl.BlockSpec(memory_space=pltpu.VMEM)
    smem = pl.BlockSpec(memory_space=pltpu.SMEM)
    dma = pltpu.SemaphoreType.DMA
    shape = (users, edge)
    return pl.pallas_call(
        functools.partial(kernel, row_count, slot_total),
        out_shape=jax.ShapeDtypeStruct(score_panel.shape, BF16),
        in_specs=[vmem, pl.BlockSpec(memory_space=pl.ANY), smem, smem, smem, vmem],
        out_specs=vmem,
        scratch_shapes=[
            pltpu.VMEM((slot_total, edge, edge), BF16),
            pltpu.VMEM((2, row_count) + shape, BF16),
            pltpu.VMEM((2,) + shape, BF16),
            pltpu.VMEM((2, levels) + shape, BF16),
            pltpu.VMEM((2, levels) + shape, BF16),
            pltpu.VMEM((2, levels) + shape, BF16),
            pltpu.VMEM((2, levels) + shape, BF16),
            pltpu.VMEM((levels,) + shape, F32),
            pltpu.VMEM((2,) + shape, F32),
            pltpu.VMEM((2,) + shape, F32),
            pltpu.VMEM((2,) + shape, F32),
            pltpu.VMEM(shape, F32),
            pltpu.SMEM((2, row_count), jnp.int32),
            pltpu.SMEM((2, row_count), F32),
            dma((slot_total,)),
            dma((2, levels)),
            dma((2, levels)),
            dma((2, levels)),
            dma((2, levels)),
            dma((2,)),
            dma((2,)),
            dma((2, levels)),
            dma((2, levels)),
            dma((2, levels)),
            dma((2, levels)),
            dma((2,)),
            dma((2,)),
        ],
        compiler_params=pltpu.CompilerParams(
            collective_id=0, has_side_effects=True, vmem_limit_bytes=56 * 1024 * 1024
        ),
    )(score_panel, blocks, block_rows, block_cols, counts, degrees)


def solution(mesh):
    in_specs = (
        P("grp", "row", "col", None, None),
        P("row", "col", None, None, None),
        P("row", "col", None),
        P("row", "col", None),
        P("row", "col"),
        P(),
    )
    out_specs = P("grp", "row", "col", None, None)
    return jax.shard_map(shards, mesh=mesh, in_specs=in_specs, out_specs=out_specs, check_vma=False)
```

time: 290 us -> 56.6 us (0.20)
  waiting for transfers between devices: 209 us -> 0 us
  Pallas kernels: 0 us -> 54.2 us
  matrix products: 31.1 us -> 0 us
  local copies, waits for them, and re-layouts: 18.2 us -> 1.57 us
  between operations: 14.3 us -> 0.66 us
  other arithmetic: 8.21 us -> 0 us
  blocking collectives: 6.61 us -> 0 us
    reduce_scatter x4 -> x0, waiting for transfers between devices: 130 us -> none  [the longest x2 130 us: column_total(): return lax.psum_scatter(col_part, 'row', scatter_dimension=1, tiled=True)]
    all_gather x2 -> x0, waiting for transfers between devices: 79.2 us -> none  [the longest x1 40.1 us: shards(): lax.all_gather(sent_second, 'row', axis=1, tiled=True)]
    pallas_call x0 -> x1, Pallas kernels: none -> 54.2 us  [shards(): pl.pallas_call(functools.partial(kernel, row_count, slot_total), out_shap...]
    dot_general x8 -> x0, matrix products: 31.1 us -> none  [the longest x2 10.5 us: local_terms(): jnp.einsum('kab,kbu->kau', tile_set, col_pick, preferred_element_type=jnp...]
    dot_general x8 -> x0, local copies, waits for them, and re-layouts: 12.7 us -> none  [the longest x2 3.81 us: local_terms(): jnp.einsum('kab,kbu->kau', tile_set, col_pick, preferred_element_type=jnp...]
    all_gather x2 -> x0, blocking collectives: 6.61 us -> none  [row_set_of(): lax.all_gather(own_sent, 'col', axis=2, tiled=True)]
    convert_element_type x4 -> x0, other arithmetic: 5.47 us -> none  [the longest x2 1.83 us: shards(): (own_inv * score_panel.astype(jnp.float32)).astype(jnp.bfloat16)]
    gather x4 -> x0, local copies, waits for them, and re-layouts: 5.44 us -> none  [the longest x2 3.94 us: local_terms(): col_pick = jnp.take(col_set, col_local, axis=0)]
  transfers between devices with their start and end apart: 6 -> 0, of which waited for: 4 -> 0; matrix products, arithmetic and copies ran while one was open for 9% -> 0% of each run, Pallas kernels for 0% -> 0%
where the time goes in v1:
time: 56.6 us; the launch traced here: 56.4 us
  Pallas kernels  54.2 us (96%)
  local copies, waits for them, and re-layouts  1.57 us (3%)
  between operations  0.66 us (1%)
    pallas_call x1, Pallas kernels, shards(): pl.pallas_call(functools.partial(kernel, row_count, slot_total), out_shap...  54.2 us
    unnamed x1, local copies, waits for them, and re-layouts  1.57 us

profile of v1, /device:TPU:1, one launch (start us, length us, event | category | flops | bytes accessed | tf_op | source)
XLA Modules:
  0.0 56.4 jit_solution(9437605792244405309)
XLA Ops:
  0.7 54.2 %shard_map.64 = bf16[1,1,1,512,128]{4,3,2,1,0:T(8,128)(2,1)} custom-call(bf16[1,1,1,512,128]{4,3,2,1,0:T(8,128)(2,1)} %panel_ref.1, bf16[1,1,8,512,512]{4,3,2,1,0:T(8,128)(2,1)} %blocks_ref.1, s32[1,1,8]{2,1,0:T(1,128)} %rows_ref.1, s32[1,1,8]{2,1,0:T(1,128)} %cols_ref.1, s32[1,1]{1,0:T(1,128)S(6)} %copy.8.counts_ref, s32[1,8,2,512]{3,2,1,0:T(2,128)} %degrees_ref.1), custom_call_target="tpu_custom_call" | custom-call | tf_op jit(solution)/shard_map/pallas_call | solution.py:300
  54.8 1.6 %copy.9 = bf16[1,1,1,512,128]{4,3,2,1,0:T(8,128)(2,1)} copy(bf16[1,1,1,512,128]{4,3,2,1,0:T(8,128)(2,1)} %shard_map.64) | data formatting | bytes 262144

commit v2 on v1

--- a/solution.py
+++ b/solution.py
@@ -64,22 +64,19 @@
     pl.semaphore_signal(barrier, inc=1, device_id={"col": mate})
     pl.semaphore_signal(barrier, inc=1, device_id={"row": y_peer})
 
-    @pl.when(z > 0)
-    def _():
-        pl.semaphore_signal(barrier, inc=1, device_id={"row": r - 2})
-
-    @pl.when(z < levels - 1)
-    def _():
-        pl.semaphore_signal(barrier, inc=1, device_id={"row": r + 2})
+    def greet(s, carry):
+        other = lax.rem(z + s, levels)
+        pl.semaphore_signal(barrier, inc=1, device_id={"row": 2 * other + y})
+        return carry
+
+    lax.fori_loop(1, levels, greet, 0)
 
     pair = degrees_ref[0, r].astype(F32)
     inv = lax.rsqrt(jnp.where(c == 0, pair[0:1], pair[1:2]))
     panel = panel_ref[0, 0, 0].astype(F32).T
     gathered[0, r] = (inv * panel).astype(BF16)
 
-    below = (z > 0).astype(jnp.int32)
-    above = (z < levels - 1).astype(jnp.int32)
-    pl.semaphore_wait(barrier, 2 + below + above)
+    pl.semaphore_wait(barrier, levels + 1)
 
     def remote(src, dst, send, recv, where):
         return pltpu.make_async_remote_copy(
@@ -87,8 +84,12 @@
         )
 
     def gather_z(a, zp):
+        ref = gathered.at[a, r]
+        return remote(ref, ref, gz_send.at[a, zp], gz_recv.at[a, z], {"row": 2 * zp + y})
+
+    def arrive_z(a, zp):
         ref = gathered.at[a, 2 * zp + y]
-        return remote(ref, ref, gz_send.at[a, zp], gz_recv.at[a, zp], {"row": r - 2})
+        return remote(ref, ref, gz_send.at[a, zp], gz_recv.at[a, zp], {"row": 2 * zp + y})
 
     def gather_y(a, zp):
         ref = gathered.at[a, 2 * zp + y]
@@ -110,7 +111,20 @@
 
     def reduce_z(a, zp):
         return remote(
-            z_out.at[a, zp], z_in.at[a, zp], rz_send.at[a, zp], rz_recv.at[a, zp], {"row": r + 2}
+            z_out.at[a, zp],
+            z_in.at[a, z],
+            rz_send.at[a, zp],
+            rz_recv.at[a, z],
+            {"row": 2 * zp + y},
+        )
+
+    def arrive_reduce(a, zp):
+        return remote(
+            z_out.at[a, zp],
+            z_in.at[a, zp],
+            rz_send.at[a, zp],
+            rz_recv.at[a, zp],
+            {"row": 2 * zp + y},
         )
 
     def reduce_m(a):
@@ -119,13 +133,15 @@
     def start_gather(a):
         gather_m(a).start()
 
-        @pl.when(z > 0)
-        def _():
-            gather_z(a, z).start()
-
         @pl.when(y == 1)
         def _():
             gather_y(a, z).start()
+
+        def down(zp, carry):
+            gather_z(a, zp).start()
+            return carry
+
+        lax.fori_loop(0, z, down, 0)
 
     start_gather(0)
 
@@ -200,26 +216,11 @@
 
         def step(s, carry):
             zp = z + s
-            gather_z(a, zp).wait_recv()
-
-            @pl.when(z > 0)
-            def _():
-                gather_z(a, zp).start()
-
+            arrive_z(a, zp).wait_recv()
             gather_y(a, zp).start()
             zq = levels - s
             reduce_y(a, zq).wait_recv()
-            summed = own_terms[zq] + y_in[a, zq].astype(F32)
-
-            @pl.when(z > 0)
-            def _():
-                reduce_z(a, zq).wait_recv()
-                z_out[a, zq] = (summed + z_in[a, zq].astype(F32)).astype(BF16)
-
-            @pl.when(z == 0)
-            def _():
-                z_out[a, zq] = summed.astype(BF16)
-
+            z_out[a, zq] = (own_terms[zq] + y_in[a, zq].astype(F32)).astype(BF16)
             reduce_z(a, zq).start()
             add_forward(a, 2 * zp + y)
 
@@ -244,10 +245,12 @@
             reduce_y(a, z).wait_recv()
             row_acc[0] += y_in[a, z].astype(F32)
 
-        @pl.when(z > 0)
-        def _():
-            reduce_z(a, z).wait_recv()
-            row_acc[0] += z_in[a, z].astype(F32)
+        def from_below(zp, carry):
+            arrive_reduce(a, zp).wait_recv()
+            row_acc[0] += z_in[a, zp].astype(F32)
+            return carry
+
+        lax.fori_loop(0, z, from_below, 0)
 
         reduce_m(a).wait_recv()
         return inv * (row_acc[0] + mate_in[a])
@@ -263,9 +266,11 @@
         gather_m(a).wait_send()
         reduce_m(a).wait_send()
 
-        @pl.when(z > 0)
-        def _():
-            gather_z(a, z).wait_send()
+        def sent_down(zp, carry):
+            gather_z(a, zp).wait_send()
+            return carry
+
+        lax.fori_loop(0, z, sent_down, 0)
 
         @pl.when(y == 1)
         def _():
@@ -276,10 +281,6 @@
             reduce_y(a, z).wait_send()
 
         def finish(zp, carry):
-            @pl.when(z > 0)
-            def _():
-                gather_z(a, zp).wait_send()
-
             gather_y(a, zp).wait_send()
             reduce_y(a, zp).wait_send()
             reduce_z(a, zp).wait_send()

time: 56.6 us -> 58.6 us (1.035)
  Pallas kernels: 54.2 us -> 56.2 us
    pallas_call x1, Pallas kernels: 54.2 us -> 56.2 us  [shards(): pl.pallas_call(functools.partial(kernel, row_count, slot_total), out_shap...]
where the time goes in v2:
time: 58.6 us; the launch traced here: 58.4 us
  Pallas kernels  56.2 us (96%)
  local copies, waits for them, and re-layouts  1.57 us (3%)
  between operations  0.66 us (1%)
    pallas_call x1, Pallas kernels, shards(): pl.pallas_call(functools.partial(kernel, row_count, slot_total), out_shap...  56.2 us
    unnamed x1, local copies, waits for them, and re-layouts  1.57 us

profile of v2, /device:TPU:1, one launch (start us, length us, event | category | flops | bytes accessed | tf_op | source)
XLA Modules:
  0.0 58.4 jit_solution(12864417079623955033)
XLA Ops:
  0.7 56.2 %shard_map.64 = bf16[1,1,1,512,128]{4,3,2,1,0:T(8,128)(2,1)} custom-call(bf16[1,1,1,512,128]{4,3,2,1,0:T(8,128)(2,1)} %panel_ref.1, bf16[1,1,8,512,512]{4,3,2,1,0:T(8,128)(2,1)} %blocks_ref.1, s32[1,1,8]{2,1,0:T(1,128)} %rows_ref.1, s32[1,1,8]{2,1,0:T(1,128)} %cols_ref.1, s32[1,1]{1,0:T(1,128)S(6)} %copy.8.counts_ref, s32[1,8,2,512]{3,2,1,0:T(2,128)} %degrees_ref.1), custom_call_target="tpu_custom_call" | custom-call | tf_op jit(solution)/shard_map/pallas_call | solution.py:301
  56.8 1.6 %copy.9 = bf16[1,1,1,512,128]{4,3,2,1,0:T(8,128)(2,1)} copy(bf16[1,1,1,512,128]{4,3,2,1,0:T(8,128)(2,1)} %shard_map.64) | data formatting | bytes 262144

commit v3 on v2

--- a/solution.py
+++ b/solution.py
@@ -33,6 +33,8 @@
     mate_out,
     mate_in,
     first_keep,
+    far_in,
+    far_got,
     slot_of,
     weight_of,
     load_sem,
@@ -48,12 +50,15 @@
     rz_recv,
     rm_send,
     rm_recv,
+    far_send,
+    far_recv,
 ):
     r = lax.axis_index("row")
     c = lax.axis_index("col")
     z = r // 2
     y = r % 2
     levels = row_count // 2
+    last = levels - 1
     y_peer = r + 1 - 2 * y
     mate = 1 - c
 
@@ -130,10 +135,28 @@
     def reduce_m(a):
         return remote(mate_out.at[a], mate_in.at[a], rm_send.at[a], rm_recv.at[a], {"col": mate})
 
+    def far_panel(a, peer):
+        ref = gathered.at[a, 2 * last + 1 - y]
+        return remote(ref, ref, far_send.at[a, 0], far_recv.at[a, 0], {"row": 2 * peer + y})
+
+    def far_term(a, peer):
+        return remote(
+            y_out.at[a, last],
+            far_in.at[a],
+            far_send.at[a, 1],
+            far_recv.at[a, 1],
+            {"row": 2 * peer + y},
+        )
+
+    def far_cross(a):
+        return remote(
+            far_in.at[a], far_got.at[a], far_send.at[a, 2], far_recv.at[a, 2], {"row": y_peer}
+        )
+
     def start_gather(a):
         gather_m(a).start()
 
-        @pl.when(y == 1)
+        @pl.when((y == 1) | (z == last))
         def _():
             gather_y(a, z).start()
 
@@ -191,7 +214,21 @@
                 row_acc[h] += term
 
     def apply(a):
+        @pl.when(z == last)
+        def _():
+            arrive_y(a, last).wait_recv()
+            far_panel(a, 0).start()
+
         gather_m(a).wait_recv()
+
+        @pl.when(z == 0)
+        def _():
+            y_out[a, last] = transposed_term(a, 2 * last + 1 - y).astype(BF16)
+            far_term(a, last).start()
+            z_out[a, last] = transposed_term(a, 2 * last + y).astype(BF16)
+            reduce_z(a, last).start()
+
+        skip = (z == 0).astype(jnp.int32)
 
         def send_terms(s, carry):
             zp = levels - 1 - s
@@ -200,7 +237,7 @@
             own_terms[zp] = transposed_term(a, 2 * zp + y)
             return carry
 
-        lax.fori_loop(0, levels - 1 - z, send_terms, 0)
+        lax.fori_loop(skip, levels - 1 - z, send_terms, 0)
 
         @pl.when(y == 0)
         def _():
@@ -209,6 +246,11 @@
 
         own_terms[z] = transposed_term(a, r)
         add_forward(a, r, fresh=True)
+
+        @pl.when(z == last)
+        def _():
+            far_term(a, 0).wait_recv()
+            far_cross(a).start()
 
         def from_peer(zp):
             arrive_y(a, zp).wait_recv()
@@ -217,11 +259,19 @@
         def step(s, carry):
             zp = z + s
             arrive_z(a, zp).wait_recv()
-            gather_y(a, zp).start()
-            zq = levels - s
-            reduce_y(a, zq).wait_recv()
-            z_out[a, zq] = (own_terms[zq] + y_in[a, zq].astype(F32)).astype(BF16)
-            reduce_z(a, zq).start()
+
+            @pl.when((z > 0) | (zp < last))
+            def _():
+                gather_y(a, zp).start()
+
+            zq = levels - s - skip
+
+            @pl.when(zq > z)
+            def _():
+                reduce_y(a, zq).wait_recv()
+                z_out[a, zq] = (own_terms[zq] + y_in[a, zq].astype(F32)).astype(BF16)
+                reduce_z(a, zq).start()
+
             add_forward(a, 2 * zp + y)
 
             @pl.when((s > 1) | (y == 0))
@@ -232,9 +282,18 @@
 
         lax.fori_loop(1, levels - z, step, 0)
 
-        @pl.when((z < levels - 1) | (y == 0))
-        def _():
-            from_peer(levels - 1)
+        @pl.when(((z > 0) & (z < last)) | ((z == last) & (y == 0)))
+        def _():
+            @pl.when(z < last)
+            def _():
+                arrive_y(a, last).wait_recv()
+
+            add_forward(a, 2 * last + 1 - y)
+
+        @pl.when(z == 0)
+        def _():
+            far_panel(a, last).wait_recv()
+            add_forward(a, 2 * last + 1 - y)
 
         mate_out[a] = row_acc[1]
         reduce_m(a).start()
@@ -251,6 +310,11 @@
             return carry
 
         lax.fori_loop(0, z, from_below, 0)
+
+        @pl.when(z == last)
+        def _():
+            far_cross(a).wait_recv()
+            row_acc[0] += far_got[a].astype(F32)
 
         reduce_m(a).wait_recv()
         return inv * (row_acc[0] + mate_in[a])
@@ -272,17 +336,29 @@
 
         lax.fori_loop(0, z, sent_down, 0)
 
-        @pl.when(y == 1)
+        @pl.when((y == 1) | (z == last))
         def _():
             gather_y(a, z).wait_send()
 
+        @pl.when(z == 0)
+        def _():
+            far_term(a, last).wait_send()
+
+        @pl.when(z == last)
+        def _():
+            far_panel(a, 0).wait_send()
+            far_cross(a).wait_send()
+
         @pl.when(y == 0)
         def _():
             reduce_y(a, z).wait_send()
 
         def finish(zp, carry):
-            gather_y(a, zp).wait_send()
-            reduce_y(a, zp).wait_send()
+            @pl.when((z > 0) | (zp < last))
+            def _():
+                gather_y(a, zp).wait_send()
+                reduce_y(a, zp).wait_send()
+
             reduce_z(a, zp).wait_send()
             return carry
 
@@ -316,6 +392,8 @@
             pltpu.VMEM((2,) + shape, F32),
             pltpu.VMEM((2,) + shape, F32),
             pltpu.VMEM(shape, F32),
+            pltpu.VMEM((2,) + shape, BF16),
+            pltpu.VMEM((2,) + shape, BF16),
             pltpu.SMEM((2, row_count), jnp.int32),
             pltpu.SMEM((2, row_count), F32),
             dma((slot_total,)),
@@ -331,6 +409,8 @@
             dma((2, levels)),
             dma((2,)),
             dma((2,)),
+            dma((2, 3)),
+            dma((2, 3)),
         ],
         compiler_params=pltpu.CompilerParams(
             collective_id=0, has_side_effects=True, vmem_limit_bytes=56 * 1024 * 1024

time: 58.6 us -> 53.6 us (0.915)
  Pallas kernels: 56.2 us -> 51.2 us
    pallas_call x1, Pallas kernels: 56.2 us -> 51.2 us  [shards(): pl.pallas_call(functools.partial(kernel, row_count, slot_total), out_shap...]
where the time goes in v3:
time: 53.6 us; the launch traced here: 53.5 us
  Pallas kernels  51.2 us (96%)
  local copies, waits for them, and re-layouts  1.57 us (3%)
  between operations  0.66 us (1%)
    pallas_call x1, Pallas kernels, shards(): pl.pallas_call(functools.partial(kernel, row_count, slot_total), out_shap...  51.2 us
    unnamed x1, local copies, waits for them, and re-layouts  1.57 us

profile of v3, /device:TPU:1, one launch (start us, length us, event | category | flops | bytes accessed | tf_op | source)
XLA Modules:
  0.0 53.5 jit_solution(1089820416259701293)
XLA Ops:
  0.7 51.2 %shard_map.64 = bf16[1,1,1,512,128]{4,3,2,1,0:T(8,128)(2,1)} custom-call(bf16[1,1,1,512,128]{4,3,2,1,0:T(8,128)(2,1)} %panel_ref.1, bf16[1,1,8,512,512]{4,3,2,1,0:T(8,128)(2,1)} %blocks_ref.1, s32[1,1,8]{2,1,0:T(1,128)} %rows_ref.1, s32[1,1,8]{2,1,0:T(1,128)} %cols_ref.1, s32[1,1]{1,0:T(1,128)S(6)} %copy.8.counts_ref, s32[1,8,2,512]{3,2,1,0:T(2,128)} %degrees_ref.1), custom_call_target="tpu_custom_call" | custom-call | tf_op jit(solution)/shard_map/pallas_call | solution.py:377
  51.9 1.6 %copy.9 = bf16[1,1,1,512,128]{4,3,2,1,0:T(8,128)(2,1)} copy(bf16[1,1,1,512,128]{4,3,2,1,0:T(8,128)(2,1)} %shard_map.64) | data formatting | bytes 262144

commit v4 on v3

--- a/solution.py
+++ b/solution.py
@@ -161,7 +161,7 @@
             gather_y(a, z).start()
 
         def down(zp, carry):
-            gather_z(a, zp).start()
+            gather_z(a, z - 1 - zp).start()
             return carry
 
         lax.fori_loop(0, z, down, 0)

time: 53.6 us -> 49.9 us (0.931)
  Pallas kernels: 51.2 us -> 47.3 us
    pallas_call x1, Pallas kernels: 51.2 us -> 47.3 us  [shards(): pl.pallas_call(functools.partial(kernel, row_count, slot_total), out_shap...]
where the time goes in v4:
time: 49.9 us; the launch traced here: 49.6 us
  Pallas kernels  47.3 us (95%)
  local copies, waits for them, and re-layouts  1.57 us (3%)
  between operations  0.66 us (1%)
    pallas_call x1, Pallas kernels, shards(): pl.pallas_call(functools.partial(kernel, row_count, slot_total), out_shap...  47.3 us
    unnamed x1, local copies, waits for them, and re-layouts  1.57 us

profile of v4, /device:TPU:1, one launch (start us, length us, event | category | flops | bytes accessed | tf_op | source)
XLA Modules:
  0.0 49.6 jit_solution(5201464737452683106)
XLA Ops:
  0.7 47.3 %shard_map.64 = bf16[1,1,1,512,128]{4,3,2,1,0:T(8,128)(2,1)} custom-call(bf16[1,1,1,512,128]{4,3,2,1,0:T(8,128)(2,1)} %panel_ref.1, bf16[1,1,8,512,512]{4,3,2,1,0:T(8,128)(2,1)} %blocks_ref.1, s32[1,1,8]{2,1,0:T(1,128)} %rows_ref.1, s32[1,1,8]{2,1,0:T(1,128)} %cols_ref.1, s32[1,1]{1,0:T(1,128)S(6)} %copy.8.counts_ref, s32[1,8,2,512]{3,2,1,0:T(2,128)} %degrees_ref.1), custom_call_target="tpu_custom_call" | custom-call | tf_op jit(solution)/shard_map/pallas_call | solution.py:377
  48.0 1.6 %copy.9 = bf16[1,1,1,512,128]{4,3,2,1,0:T(8,128)(2,1)} copy(bf16[1,1,1,512,128]{4,3,2,1,0:T(8,128)(2,1)} %shard_map.64) | data formatting | bytes 262144

commit v5 on v4

--- a/solution.py
+++ b/solution.py
@@ -52,6 +52,7 @@
     rm_recv,
     far_send,
     far_recv,
+    hub_send,
 ):
     r = lax.axis_index("row")
     c = lax.axis_index("col")
@@ -59,6 +60,7 @@
     y = r % 2
     levels = row_count // 2
     last = levels - 1
+    at_last = (z == last).astype(jnp.int32)
     y_peer = r + 1 - 2 * y
     mate = 1 - c
 
@@ -139,6 +141,11 @@
         ref = gathered.at[a, 2 * last + 1 - y]
         return remote(ref, ref, far_send.at[a, 0], far_recv.at[a, 0], {"row": 2 * peer + y})
 
+    def hub_panel(a, which):
+        ref = gathered.at[a, 2 * last + (y if which == 0 else 1 - y)]
+        recv = gz_recv.at[a, last] if which == 0 else far_recv.at[a, 0]
+        return remote(ref, ref, hub_send.at[a, which], recv, {"row": y})
+
     def far_term(a, peer):
         return remote(
             y_out.at[a, last],
@@ -164,7 +171,7 @@
             gather_z(a, z - 1 - zp).start()
             return carry
 
-        lax.fori_loop(0, z, down, 0)
+        lax.fori_loop(0, z - at_last, down, 0)
 
     start_gather(0)
 
@@ -217,7 +224,7 @@
         @pl.when(z == last)
         def _():
             arrive_y(a, last).wait_recv()
-            far_panel(a, 0).start()
+            far_panel(a, 1).start()
 
         gather_m(a).wait_recv()
 
@@ -260,9 +267,15 @@
             zp = z + s
             arrive_z(a, zp).wait_recv()
 
-            @pl.when((z > 0) | (zp < last))
+            @pl.when((z > 1) | (zp < last))
             def _():
                 gather_y(a, zp).start()
+
+            @pl.when((z == 1) & (zp == last))
+            def _():
+                hub_panel(a, 0).start()
+                far_panel(a, last).wait_recv()
+                hub_panel(a, 1).start()
 
             zq = levels - s - skip
 
@@ -284,7 +297,7 @@
 
         @pl.when(((z > 0) & (z < last)) | ((z == last) & (y == 0)))
         def _():
-            @pl.when(z < last)
+            @pl.when((z > 1) & (z < last))
             def _():
                 arrive_y(a, last).wait_recv()
 
@@ -334,7 +347,7 @@
             gather_z(a, zp).wait_send()
             return carry
 
-        lax.fori_loop(0, z, sent_down, 0)
+        lax.fori_loop(at_last, z, sent_down, 0)
 
         @pl.when((y == 1) | (z == last))
         def _():
@@ -344,9 +357,14 @@
         def _():
             far_term(a, last).wait_send()
 
+        @pl.when(z == 1)
+        def _():
+            hub_panel(a, 0).wait_send()
+            hub_panel(a, 1).wait_send()
+
         @pl.when(z == last)
         def _():
-            far_panel(a, 0).wait_send()
+            far_panel(a, 1).wait_send()
             far_cross(a).wait_send()
 
         @pl.when(y == 0)
@@ -354,9 +372,12 @@
             reduce_y(a, z).wait_send()
 
         def finish(zp, carry):
+            @pl.when((z > 1) | (zp < last))
+            def _():
+                gather_y(a, zp).wait_send()
+
             @pl.when((z > 0) | (zp < last))
             def _():
-                gather_y(a, zp).wait_send()
                 reduce_y(a, zp).wait_send()
 
             reduce_z(a, zp).wait_send()
@@ -411,6 +432,7 @@
             dma((2,)),
             dma((2, 3)),
             dma((2, 3)),
+            dma((2, 2)),
         ],
         compiler_params=pltpu.CompilerParams(
             collective_id=0, has_side_effects=True, vmem_limit_bytes=56 * 1024 * 1024

time: 49.9 us -> 48.4 us (0.970)
  Pallas kernels: 47.3 us -> 46 us
    pallas_call x1, Pallas kernels: 47.3 us -> 46 us  [shards(): pl.pallas_call(functools.partial(kernel, row_count, slot_total), out_shap...]
where the time goes in v5:
time: 48.4 us; the launch traced here: 48.3 us
  Pallas kernels  46 us (95%)
  local copies, waits for them, and re-layouts  1.57 us (3%)
  between operations  0.66 us (1%)
    pallas_call x1, Pallas kernels, shards(): pl.pallas_call(functools.partial(kernel, row_count, slot_total), out_shap...  46 us
    unnamed x1, local copies, waits for them, and re-layouts  1.57 us

profile of v5, /device:TPU:1, one launch (start us, length us, event | category | flops | bytes accessed | tf_op | source)
XLA Modules:
  0.0 48.3 jit_solution(105510671229626088)
XLA Ops:
  0.7 46.0 %shard_map.64 = bf16[1,1,1,512,128]{4,3,2,1,0:T(8,128)(2,1)} custom-call(bf16[1,1,1,512,128]{4,3,2,1,0:T(8,128)(2,1)} %panel_ref.1, bf16[1,1,8,512,512]{4,3,2,1,0:T(8,128)(2,1)} %blocks_ref.1, s32[1,1,8]{2,1,0:T(1,128)} %rows_ref.1, s32[1,1,8]{2,1,0:T(1,128)} %cols_ref.1, s32[1,1]{1,0:T(1,128)S(6)} %copy.8.counts_ref, s32[1,8,2,512]{3,2,1,0:T(2,128)} %degrees_ref.1), custom_call_target="tpu_custom_call" | custom-call | tf_op jit(solution)/shard_map/pallas_call | solution.py:398
  46.7 1.6 %copy.9 = bf16[1,1,1,512,128]{4,3,2,1,0:T(8,128)(2,1)} copy(bf16[1,1,1,512,128]{4,3,2,1,0:T(8,128)(2,1)} %shard_map.64) | data formatting | bytes 262144
